TPU v7x, 32 devices: a whole 2x2x4 slice. The times are simulated.
32 devices in a mesh: grp: 2 (over x), tile: 16 (over z, y, core).
Axes of the slice: x: 2, y: 2, z: 4, core: 2. Of those that a mesh axis runs over, the one named last changes fastest.
Arguments:
- ocean_anom: bfloat16 [1024, 80, 256], P(('grp', 'tile')), parts along dimension 0, may hold values from -6 to 6
- ocean_innov: bfloat16 [1024, 256], P(('grp', 'tile')), parts along dimension 0, may hold values from -6 to 6
- ocean_mean: float32 [1024, 256], P(('grp', 'tile')), parts along dimension 0, may hold values from -6 to 6
- atm_anom: bfloat16 [1024, 80, 256], P(('grp', 'tile')), parts along dimension 0, may hold values from -6 to 6
- atm_innov: bfloat16 [1024, 256], P(('grp', 'tile')), parts along dimension 0, may hold values from -6 to 6
- atm_mean: float32 [1024, 256], P(('grp', 'tile')), parts along dimension 0, may hold values from -6 to 6
- air_temp: float32 [512, 512], P(('grp', 'tile')), parts along dimension 0, may hold values from -6 to 6
- pair_owner: int32 [2048, 1], P('tile'), may hold values from 0 to 15; in each aligned block of 128 rows (0 to 127, 128 to 255, ...) at most 12 rows name the same one
- pair_slot: int32 [2048], P('tile'), may hold values from 0 to 31
- pair_ocean: int32 [2048], P('tile'), may hold values from 0 to 31
- pair_shift: int32 [2048, 2], P('tile'), may hold values from -8 to 8
Outputs:
- atm_analysis: float32 [1024, 256], P(('grp', 'tile')), parts along dimension 0
- ocean_next: float32 [512, 512], P(('grp', 'tile')), parts along dimension 0
There are 2 independent parts, one for each index of `grp`. A program takes and returns all parts, laid end to end along the dimension named above; an argument that names none is the same for every part. Nothing has to cross between parts.
Inputs may be any that keep to these rules, and one draw needn't show every extreme that they name: `pair_owner`: in the rows of one device no device number appears more than 12 times, and some device number appears exactly 12 times.
All inputs are finite; a program needn't handle non-finite values.
Results may differ from a plain program's by a relative error of at most 0.0003.
The roundings to bfloat16 on the way count: a program that leaves them out, or rounds other values in their place, can miss the bound.
Values may be sent and summed in bfloat16 or wider, within the bound.
A program may use at most 128 MiB of HBM per device.

v0:
```python
import math

import jax
import jax.numpy as jnp
from jax import lax
from jax.sharding import PartitionSpec as P

SIDE = 16
RADIUS = 4


diffusion_rate = 0.2
relax_rate = 0.25


def padded_2(shard, sides, width):
    for axis, dim in sides:
        peers, length = (lax.axis_size(axis), shard.shape[dim])
        up = [(i, (i + 1) % peers) for i in range(peers)]
        down = [(j, i) for i, j in up]
        last = lax.slice_in_dim(shard, length - width, length, axis=dim)
        initial = lax.slice_in_dim(shard, 0, width, axis=dim)
        before = lax.ppermute(last, axis, up)
        after = lax.ppermute(initial, axis, down)
        shard = jnp.concatenate([before, shard, after], axis=dim)
    return shard


def taper_table(shift_x, shift_y):
    cell_index = jnp.arange(SIDE * SIDE, dtype=jnp.int32)
    column = cell_index // SIDE
    row_index = cell_index % SIDE
    delta_x = (column[:, None] + shift_x - column[None, :]).astype(jnp.float32)
    delta_y = (row_index[:, None] + shift_y - row_index[None, :]).astype(jnp.float32)
    radius = jnp.sqrt(delta_x * delta_x + delta_y * delta_y) / RADIUS
    inner_part = (
        ((-0.25 * radius + 0.5) * radius + 0.625) * radius - 5.0 / 3.0
    ) * radius * radius + 1.0
    safe_radius = jnp.maximum(radius, 1.0)
    outer_part = (
        (
            (((safe_radius / 12.0 - 0.5) * safe_radius + 0.625) * safe_radius + 5.0 / 3.0)
            * safe_radius
            - 5.0
        )
        * safe_radius
        + 4.0
        - 2.0 / (3.0 * safe_radius)
    )
    weight = jnp.where(radius <= 1.0, inner_part, jnp.where(radius < 2.0, outer_part, 0.0))
    return weight.astype(jnp.bfloat16)


def scaled(anomalies, innovation):
    return (anomalies.astype(jnp.float32) * innovation.astype(jnp.float32)[..., None, :]).astype(
        jnp.bfloat16
    )


def self_term(anomalies, weighted, table):
    members = anomalies.shape[1]
    towards = jnp.dot(
        weighted.reshape(-1, table.shape[0]), table, preferred_element_type=jnp.float32
    )
    towards = towards.reshape(anomalies.shape)
    return jnp.sum(anomalies.astype(jnp.float32) * towards, axis=1) / (members - 1)


def cross_terms(ocean_part, ocean_weighted, atm_part, atm_weighted, tables):
    members = ocean_part.shape[1]
    towards_ocean = jnp.einsum(
        "bki,bij->bkj", atm_weighted, tables, preferred_element_type=jnp.float32
    )
    ocean_terms = jnp.sum(ocean_part.astype(jnp.float32) * towards_ocean, axis=1) / (members - 1)
    towards_atm = jnp.einsum(
        "bkj,bij->bki", ocean_weighted, tables, preferred_element_type=jnp.float32
    )
    atm_terms = jnp.sum(atm_part.astype(jnp.float32) * towards_atm, axis=1) / (members - 1)
    return (ocean_terms, atm_terms)


def local(
    ocean_anom,
    ocean_innov,
    ocean_mean,
    atm_anom,
    atm_innov,
    atm_mean,
    air_temp,
    pair_owner,
    pair_slot,
    pair_ocean,
    pair_shift,
):
    peers = lax.axis_size("tile")
    listed_pairs = pair_slot.shape[0]
    capacity = max(2, 3 * listed_pairs // (2 * peers))
    slot_total = peers * capacity
    members = ocean_anom.shape[1]
    cell_total = ocean_anom.shape[2]
    ocean_tiles = ocean_anom.shape[0]
    ocean_scaled = scaled(ocean_anom, ocean_innov)
    atm_scaled = scaled(atm_anom, atm_innov)
    self_table = taper_table(jnp.int32(0), jnp.int32(0))
    ocean_inc = self_term(ocean_anom, ocean_scaled, self_table)
    atm_inc = self_term(atm_anom, atm_scaled, self_table)
    owners = pair_owner[:, 0]
    position = jnp.arange(listed_pairs, dtype=jnp.int32)
    earlier = (owners[:, None] == owners[None, :]) & (position[None, :] < position[:, None])
    slot_index = owners * capacity + jnp.sum(earlier, axis=1)
    request_rows = jnp.stack(
        [jnp.ones_like(owners), pair_slot, pair_shift[:, 0], pair_shift[:, 1]], axis=1
    )
    request = jnp.zeros((slot_total, 4), jnp.int32).at[slot_index].set(request_rows)
    arrived = lax.all_to_all(request, "tile", split_axis=0, concat_axis=0, tiled=True)
    slot_live = (arrived[:, 0] == 1).astype(jnp.float32)
    asked_tiles = arrived[:, 1]
    shipped = (
        jnp.zeros((slot_total, members, cell_total), jnp.bfloat16)
        .at[slot_index]
        .set(ocean_anom[pair_ocean])
    )
    shipped_innov = (
        jnp.zeros((slot_total, cell_total), jnp.bfloat16)
        .at[slot_index]
        .set(ocean_innov[pair_ocean])
    )
    got_anom, got_innov = (
        lax.all_to_all(shipped, "tile", split_axis=0, concat_axis=0, tiled=True),
        lax.all_to_all(shipped_innov, "tile", split_axis=0, concat_axis=0, tiled=True),
    )

    def visiting(block_items):
        anom_rows, innov_rows, asked = block_items
        tables = jax.vmap(taper_table)(asked[:, 2], asked[:, 3])
        atm_rows = asked[:, 1]
        return cross_terms(
            anom_rows,
            scaled(anom_rows, innov_rows),
            atm_anom[atm_rows],
            atm_scaled[atm_rows],
            tables,
        )

    group = math.gcd(slot_total, 64)
    ocean_terms, atm_terms = lax.map(
        visiting,
        (
            got_anom.reshape(-1, group, members, cell_total),
            got_innov.reshape(-1, group, cell_total),
            arrived.reshape(-1, group, 4),
        ),
    )
    atm_inc = atm_inc.at[asked_tiles].add(
        atm_terms.reshape(slot_total, cell_total) * slot_live[:, None]
    )
    returned = lax.all_to_all(
        ocean_terms.reshape(slot_total, cell_total), "tile", split_axis=0, concat_axis=0, tiled=True
    )
    ocean_inc = ocean_inc.at[pair_ocean].add(returned[slot_index])
    atm_analysis = atm_mean + atm_inc
    side_cells = air_temp.shape[0]
    ocean_grid = (
        (ocean_mean + ocean_inc)
        .reshape(ocean_tiles, side_cells, side_cells)
        .transpose(1, 0, 2)
        .reshape(side_cells, ocean_tiles * side_cells)
    )
    extended = padded_2(ocean_grid, (("tile", 0),), 1)
    padded = jnp.pad(extended, ((0, 0), (1, 1)), mode="edge")
    laplace = (
        padded[2:, 1:-1]
        + padded[:-2, 1:-1]
        + padded[1:-1, 2:]
        + padded[1:-1, :-2]
        - 4.0 * ocean_grid
    )
    ocean_next = ocean_grid + diffusion_rate * laplace + relax_rate * (air_temp - ocean_grid)
    return (atm_analysis, ocean_next)


def solution(mesh):
    return jax.shard_map(
        local,
        mesh=mesh,
        in_specs=(
            P(("grp", "tile"), None, None),
            P(("grp", "tile"), None),
            P(("grp", "tile"), None),
            P(("grp", "tile"), None, None),
            P(("grp", "tile"), None),
            P(("grp", "tile"), None),
            P(("grp", "tile"), None),
            P("tile", None),
            P("tile"),
            P("tile"),
            P("tile", None),
        ),
        out_specs=(P(("grp", "tile"), None), P(("grp", "tile"), None)),
        check_vma=False,
    )
```

profile of v0, /device:TPU:0, one launch (start us, length us, event | category | flops | bytes accessed | tf_op | source)
XLA Modules:
  0.0 459.5 jit_solution(6079777204059781877)
XLA Ops:
  4.8 7.4 %all-to-all-start = ((s32[16,12,4]{1,2,0:T(4,128)}), s32[16,12,4]{1,2,0:T(4,128)S(1)}, u32[]{:S(2)}, u32[]{:S(2)}) async-start(s32[16,12,4]{1,2,0:T(4,128)} %copy.33), calls=%async_computation | async-start | bytes 65536 | tf_op jit(solution)/shard_map/all_to_all | solution.py:115
  12.9 2.5 scatter_custom_fusion.2
  16.0 2.8 all-to-all-done
  18.8 3.5 all-to-all-start.2
  22.3 4.5 gather_fusion.2
  26.8 3.7 broadcast_in_dim.22
  30.5 20.4 %scatter_fusion = bf16[192,80,256]{2,1,0:T(8,128)(2,1)} fusion(bf16[192,80,256]{2,1,0:T(8,128)(2,1)} %broadcast_in_dim.22, s32[128]{0:T(128)S(1)} %fusion.107, bf16[128,80,256]{2,1,0:T(8,128)(2,1)} %gather_fusion.2), kind=kCustom, calls=%fused_computation.6 | custom fusion | bytes 15729152 | tf_op jit(solution)/shard_map/scatter | solution.py:121
  51.0 6.4 %all-to-all-start.1 = ((bf16[192,80,256]{2,1,0:T(8,128)(2,1)}), bf16[192,80,256]{2,1,0:T(8,128)(2,1)}, u32[]{:S(2)}, u32[]{:S(2)}) async-start(bf16[192,80,256]{2,1,0:T(8,128)(2,1)} %scatter_fusion), calls=%async_computation.1 | async-start | bytes 15728640 | tf_op jit(solution)/shard_map/all_to_all | solution.py:129
  62.6 136.4 %all-to-all-done.1 = bf16[192,80,256]{2,1,0:T(8,128)(2,1)} async-done(((bf16[192,80,256]{2,1,0:T(8,128)(2,1)}), bf16[192,80,256]{2,1,0:T(8,128)(2,1)}, u32[]{:S(2)}, u32[]{:S(2)}) %all-to-all-start.1) | async-done | bytes 7864352 | tf_op jit(solution)/shard_map/all_to_all | solution.py:129
  198.9 205.1 %while.14 = (s32[]{:T(128)}, f32[3,64,256]{2,1,0:T(8,128)S(1)}, f32[3,64,256]{2,1,0:T(8,128)S(1)}, bf16[3,64,80,256]{3,2,1,0:T(8,128)(2,1)}, s32[3,64,4]{1,0,2:T...) while((s32[]{:T(128)}, f32[3,64,256]{2,1,0:T(8,128)S(1)}, ...), condition=%wide.region_8.9_spmd, body=%wide.region_5.8_spmd.sunk | while | flops 1656017664 | bytes 27181936 | solution.py:146
  199.0 3.9 fusion.159
  205.4 29.8 %multiply_reduce_fusion.2 = f32[64,256]{1,0:T(8,128)S(1)} fusion(bf16[64,80,256]{2,1,0:T(8,128)(2,1)} %gather_fusion, s32[256]{0:T(256)S(1)} %and_select_fusion.6, s32[64,256]{1,0:T(8,128)S(1)} %broadcast_add_fusion.4, s32[256]{0:T(256)S(1)} %and_select_fusion.7, s32[64,256]{1,0:T(8,128)S(1)} %broadcast_add_fusion.5, bf16[64,80,256]{2,1,0:T(8,128)(2,1)} %fusion.159), kind=kOutput, calls=%fused_computation.32.clone.3 | convolution fusion | flops 825999360 | bytes 5441536 | tf_op jit(solution)/shard_map/while/body/eval_jaxpr/bkj,bij->bki/dot_general | solution.py:75
  237.5 29.8 %fusion.160 = f32[64,256]{1,0:T(8,128)S(1)} fusion(bf16[3,64,80,256]{3,2,1,0:T(8,128)(2,1)} %get-tuple-element.242, s32[]{:T(128)} %get-tuple-element.230, bf16[64,80,256]{2,1,0:T(8,128)(2,1)} %gather_fusion.1, s32[256]{0:T(256)S(1)} %and_select_fusion.6, s32[64,256]{1,0:T(8,128)S(1)} %broadcast_add_fusion.4, s32[256]{0:T(256)S(1)} %and_select_fusion.7, ...), kind=kOutput, calls=%fused_computation.30.clone.2 | convolution fusion | flops 825999360 | bytes 5441540 | tf_op jit(solution)/shard_map/while/body/eval_jaxpr/bki,bij->bkj/dot_general | solution.py:71
  267.3 3.9 fusion.159
  271.5 2.3 gather_fusion
  273.8 29.8 %multiply_reduce_fusion.2 = f32[64,256]{1,0:T(8,128)S(1)} fusion(bf16[64,80,256]{2,1,0:T(8,128)(2,1)} %gather_fusion, s32[256]{0:T(256)S(1)} %and_select_fusion.6, s32[64,256]{1,0:T(8,128)S(1)} %broadcast_add_fusion.4, s32[256]{0:T(256)S(1)} %and_select_fusion.7, s32[64,256]{1,0:T(8,128)S(1)} %broadcast_add_fusion.5, bf16[64,80,256]{2,1,0:T(8,128)(2,1)} %fusion.159), kind=kOutput, calls=%fused_computation.32.clone.3 | convolution fusion | flops 825999360 | bytes 5441536 | tf_op jit(solution)/shard_map/while/body/eval_jaxpr/bkj,bij->bki/dot_general | solution.py:75
  303.6 2.3 gather_fusion.1
  305.9 29.8 %fusion.160 = f32[64,256]{1,0:T(8,128)S(1)} fusion(bf16[3,64,80,256]{3,2,1,0:T(8,128)(2,1)} %get-tuple-element.242, s32[]{:T(128)} %get-tuple-element.230, bf16[64,80,256]{2,1,0:T(8,128)(2,1)} %gather_fusion.1, s32[256]{0:T(256)S(1)} %and_select_fusion.6, s32[64,256]{1,0:T(8,128)S(1)} %broadcast_add_fusion.4, s32[256]{0:T(256)S(1)} %and_select_fusion.7, ...), kind=kOutput, calls=%fused_computation.30.clone.2 | convolution fusion | flops 825999360 | bytes 5441540 | tf_op jit(solution)/shard_map/while/body/eval_jaxpr/bki,bij->bkj/dot_general | solution.py:71
  335.7 3.9 fusion.159
  342.1 29.8 %multiply_reduce_fusion.2 = f32[64,256]{1,0:T(8,128)S(1)} fusion(bf16[64,80,256]{2,1,0:T(8,128)(2,1)} %gather_fusion, s32[256]{0:T(256)S(1)} %and_select_fusion.6, s32[64,256]{1,0:T(8,128)S(1)} %broadcast_add_fusion.4, s32[256]{0:T(256)S(1)} %and_select_fusion.7, s32[64,256]{1,0:T(8,128)S(1)} %broadcast_add_fusion.5, bf16[64,80,256]{2,1,0:T(8,128)(2,1)} %fusion.159), kind=kOutput, calls=%fused_computation.32.clone.3 | convolution fusion | flops 825999360 | bytes 5441536 | tf_op jit(solution)/shard_map/while/body/eval_jaxpr/bkj,bij->bki/dot_general | solution.py:75
  374.2 29.8 %fusion.160 = f32[64,256]{1,0:T(8,128)S(1)} fusion(bf16[3,64,80,256]{3,2,1,0:T(8,128)(2,1)} %get-tuple-element.242, s32[]{:T(128)} %get-tuple-element.230, bf16[64,80,256]{2,1,0:T(8,128)(2,1)} %gather_fusion.1, s32[256]{0:T(256)S(1)} %and_select_fusion.6, s32[64,256]{1,0:T(8,128)S(1)} %broadcast_add_fusion.4, s32[256]{0:T(256)S(1)} %and_select_fusion.7, ...), kind=kOutput, calls=%fused_computation.30.clone.2 | convolution fusion | flops 825999360 | bytes 5441540 | tf_op jit(solution)/shard_map/while/body/eval_jaxpr/bki,bij->bkj/dot_general | solution.py:71
  404.8 34.4 %all-to-all-start.3 = ((f32[16,12,256]{2,1,0:T(8,128)}), f32[16,12,256]{2,1,0:T(8,128)S(1)}, u32[]{:S(2)}, u32[]{:S(2)}) async-start(f32[16,12,256]{2,1,0:T(8,128)} %all_to_all.31), calls=%async_computation.3 | async-start | bytes 524288 | tf_op jit(solution)/shard_map/all_to_all | solution.py:157
  439.2 10.0 %all-to-all-done.3 = f32[16,12,256]{2,1,0:T(8,128)S(1)} async-done(((f32[16,12,256]{2,1,0:T(8,128)}), f32[16,12,256]{2,1,0:T(8,128)S(1)}, u32[]{:S(2)}, u32[]{:S(2)}) %all-to-all-start.3) | async-done | bytes 196640 | tf_op jit(solution)/shard_map/all_to_all | solution.py:157
  455.1 3.6 collective-permute-done.1
  (102 shorter events, 27.6 us)
Async XLA Ops:
  4.8 14.0 %all-to-all-start = ((s32[16,12,4]{1,2,0:T(4,128)}), s32[16,12,4]{1,2,0:T(4,128)S(1)}, u32[]{:S(2)}, u32[]{:S(2)}) async-start(s32[16,12,4]{1,2,0:T(4,128)} %copy.33), calls=%async_computation | async-start | bytes 65536 | tf_op jit(solution)/shard_map/all_to_all | solution.py:115
  12.8 17.7 %copy-start.11 = (s32[128]{0:T(128)}, s32[128]{0:T(128)S(1)}, u32[]{:S(2)}) copy-start(s32[128]{0:T(128)S(1)} %compare_select_fusion.2) | copy-start | bytes 1540
  18.8 32.1 %all-to-all-start.2 = ((bf16[16,12,256]{2,1,0:T(8,128)(2,1)}), bf16[16,12,256]{2,1,0:T(8,128)(2,1)S(1)}, u32[]{:S(2)}, u32[]{:S(2)}) async-start(bf16[16,12,256]{2,1,0:T(8,128)(2,1)} %all_to_all.29), calls=%async_computation.2 | async-start | bytes 262144 | tf_op jit(solution)/shard_map/all_to_all | solution.py:130
  50.9 6.4 %copy-start.8 = (bf16[32,256]{1,0:T(8,128)(2,1)S(1)}, bf16[32,256]{1,0:T(8,128)(2,1)}, u32[]{:S(2)}) copy-start(bf16[32,256]{1,0:T(8,128)(2,1)} %param.14) | copy-start | bytes 49156
  50.9 6.5 %copy-start.9 = (bf16[32,256]{1,0:T(8,128)(2,1)S(1)}, bf16[32,256]{1,0:T(8,128)(2,1)}, u32[]{:S(2)}) copy-start(bf16[32,256]{1,0:T(8,128)(2,1)} %param.17) | copy-start | bytes 49156
  50.9 7.1 %copy-start.3 = (bf16[32,80,256]{2,1,0:T(8,128)(2,1)S(1)}, bf16[32,80,256]{2,1,0:T(8,128)(2,1)}, u32[]{:S(2)}) copy-start(bf16[32,80,256]{2,1,0:T(8,128)(2,1)} %param.13) | copy-start | bytes 3932164
  50.9 8.1 %copy-start.5 = (f32[32,256]{1,0:T(8,128)S(1)}, f32[32,256]{1,0:T(8,128)}, u32[]{:S(2)}) copy-start(f32[32,256]{1,0:T(8,128)} %param.15) | copy-start | bytes 98308
  50.9 8.8 %copy-start = (bf16[32,80,256]{2,1,0:T(8,128)(2,1)S(1)}, bf16[32,80,256]{2,1,0:T(8,128)(2,1)}, u32[]{:S(2)}) copy-start(bf16[32,80,256]{2,1,0:T(8,128)(2,1)} %param.16) | copy-start | bytes 3932164
  51.0 147.9 %all-to-all-start.1 = ((bf16[192,80,256]{2,1,0:T(8,128)(2,1)}), bf16[192,80,256]{2,1,0:T(8,128)(2,1)}, u32[]{:S(2)}, u32[]{:S(2)}) async-start(bf16[192,80,256]{2,1,0:T(8,128)(2,1)} %scatter_fusion), calls=%async_computation.1 | async-start | bytes 15728640 | tf_op jit(solution)/shard_map/all_to_all | solution.py:129
  57.3 3.4 copy-start.6
  198.9 240.3 %copy-start.10 = (s32[192,4]{0,1:T(4,128)S(1)}, s32[192,4]{0,1:T(4,128)}, u32[]{:S(2)}) copy-start(s32[192,4]{0,1:T(4,128)} %all_to_all.27) | copy-start | bytes 9220
  198.9 250.3 %copy-start.4 = (f32[32,256]{1,0:T(8,128)S(1)}, f32[32,256]{1,0:T(8,128)}, u32[]{:S(2)}) copy-start(f32[32,256]{1,0:T(8,128)} %multiply_add_fusion) | copy-start | bytes 98308
  198.9 254.2 %copy-start.1 = (f32[32,256]{1,0:T(8,128)S(1)}, f32[32,256]{1,0:T(8,128)}, u32[]{:S(2)}) copy-start(f32[32,256]{1,0:T(8,128)} %multiply_add_fusion.1) | copy-start | bytes 98308
  198.9 259.8 %copy-start.7 = (f32[16,512]{1,0:T(8,128)S(1)}, f32[16,512]{1,0:T(8,128)}, u32[]{:S(2)}) copy-start(f32[16,512]{1,0:T(8,128)} %param.19) | copy-start | bytes 98308
  404.8 44.4 %all-to-all-start.3 = ((f32[16,12,256]{2,1,0:T(8,128)}), f32[16,12,256]{2,1,0:T(8,128)S(1)}, u32[]{:S(2)}, u32[]{:S(2)}) async-start(f32[16,12,256]{2,1,0:T(8,128)} %all_to_all.31), calls=%async_computation.3 | async-start | bytes 524288 | tf_op jit(solution)/shard_map/all_to_all | solution.py:157
  451.5 3.6 collective-permute-start
  453.0 5.7 %collective-permute-start.1 = (f32[1,512]{1,0:T(1,128)S(1)}, f32[1,512]{1,0:T(1,128)S(1)}, u32[]{:S(2)}, u32[]{:S(2)}) collective-permute-start(f32[1,512]{1,0:T(1,128)S(1)} %slice.75), channel_id=1, source_target_pairs={{0,1},{1,2},{2,3},{3,4},{4,5},{5,6},{6,7},{7,8},{8,9},{9,10},{10,1... | collective-permute-start | bytes 6152 | tf_op jit(solution)/shard_map/ppermute | solution.py:23
  454.8 4.6 %copy-start.2 = (f32[32,256]{1,0:T(8,128)}, f32[32,256]{1,0:T(8,128)S(1)}, u32[]{:S(2)}) copy-start(f32[32,256]{1,0:T(8,128)S(1)} %scatter_fusion.1) | copy-start | bytes 98308
where the time goes:
time: 460 us; the launch traced here: 459 us
  matrix products  181 us (39%)
  waiting for transfers between devices  153 us (33%)
  starting transfers between devices  53 us (12%)
  local copies, waits for them, and re-layouts  49.5 us (11%)
  other arithmetic  22.1 us (5%)
    all_to_all x1, waiting for transfers between devices, local(): lax.all_to_all(shipped, 'tile', split_axis=0, concat_axis=0, tiled=True)  136 us
    dot_general x3, matrix products, cross_terms(): jnp.einsum('bkj,bij->bki', ocean_weighted, tables, preferred_element_type...  89.5 us
    dot_general x3, matrix products, cross_terms(): jnp.einsum('bki,bij->bkj', atm_weighted, tables, preferred_element_type=j...  89.4 us
    all_to_all x1, starting transfers between devices, local(): lax.all_to_all(ocean_terms.reshape(slot_total, cell_total), 'tile', split...  34.4 us
    scatter x1, local copies, waits for them, and re-layouts, local(): shipped = jnp.zeros((slot_total, members, cell_total), jnp.bfloat16).at[s...  20.4 us
    dot_general x3, other arithmetic, cross_terms(): jnp.einsum('bkj,bij->bki', ocean_weighted, tables, preferred_element_type...  11.8 us
    all_to_all x1, waiting for transfers between devices, local(): lax.all_to_all(ocean_terms.reshape(slot_total, cell_total), 'tile', split...  10 us
  transfers between devices with their start and end apart: 6, of which 4 were waited for; matrix products, arithmetic and copies ran while one was open for 8% of the time, Pallas kernels for 0%

commit v1 on v0

--- a/solution.py
+++ b/solution.py
@@ -1,8 +1,8 @@
-import math
-
 import jax
 import jax.numpy as jnp
 from jax import lax
+from jax.experimental import pallas as pl
+from jax.experimental.pallas import tpu as pltpu
 from jax.sharding import PartitionSpec as P
 
 SIDE = 16
@@ -26,12 +26,28 @@
     return shard
 
 
+SHIFT_MAX = 8
+
+
 def taper_table(shift_x, shift_y):
     cell_index = jnp.arange(SIDE * SIDE, dtype=jnp.int32)
     column = cell_index // SIDE
     row_index = cell_index % SIDE
     delta_x = (column[:, None] + shift_x - column[None, :]).astype(jnp.float32)
     delta_y = (row_index[:, None] + shift_y - row_index[None, :]).astype(jnp.float32)
+    return taper(delta_x, delta_y)
+
+
+def taper_strips():
+    rows = jnp.arange((SIDE + 2 * SHIFT_MAX) * SIDE, dtype=jnp.int32)[None, :, None]
+    cols = jnp.arange(SIDE * SIDE, dtype=jnp.int32)[None, None, :]
+    sy = jnp.arange(2 * SHIFT_MAX + 1, dtype=jnp.int32)[:, None, None] - SHIFT_MAX
+    delta_x = (rows // SIDE - SHIFT_MAX - cols // SIDE + 0 * sy).astype(jnp.float32)
+    delta_y = (rows % SIDE + sy - cols % SIDE).astype(jnp.float32)
+    return taper(delta_x, delta_y)
+
+
+def taper(delta_x, delta_y):
     radius = jnp.sqrt(delta_x * delta_x + delta_y * delta_y) / RADIUS
     inner_part = (
         ((-0.25 * radius + 0.5) * radius + 0.625) * radius - 5.0 / 3.0
@@ -66,17 +82,50 @@
     return jnp.sum(anomalies.astype(jnp.float32) * towards, axis=1) / (members - 1)
 
 
-def cross_terms(ocean_part, ocean_weighted, atm_part, atm_weighted, tables):
-    members = ocean_part.shape[1]
-    towards_ocean = jnp.einsum(
-        "bki,bij->bkj", atm_weighted, tables, preferred_element_type=jnp.float32
-    )
-    ocean_terms = jnp.sum(ocean_part.astype(jnp.float32) * towards_ocean, axis=1) / (members - 1)
-    towards_atm = jnp.einsum(
-        "bkj,bij->bki", ocean_weighted, tables, preferred_element_type=jnp.float32
-    )
-    atm_terms = jnp.sum(atm_part.astype(jnp.float32) * towards_atm, axis=1) / (members - 1)
-    return (ocean_terms, atm_terms)
+GROUP = 8
+
+
+def pair_kernel(asked, anom, innov, atm, atm_scaled, strips, ocean_out, atm_out):
+    step = pl.program_id(0)
+    members = anom.shape[1]
+    cells = SIDE * SIDE
+    for g in range(GROUP):
+        base = (step * GROUP + g) * 4
+        slot = asked[base + 1]
+        sx = asked[base + 2]
+        sy = asked[base + 3]
+        there = strips[sy + SHIFT_MAX, pl.ds(pl.multiple_of((sx + SHIFT_MAX) * SIDE, SIDE), cells), :]
+        back = strips[SHIFT_MAX - sy, pl.ds(pl.multiple_of((SHIFT_MAX - sx) * SIDE, SIDE), cells), :]
+        ocean = anom[g].astype(jnp.float32)
+        ocean_scaled = (ocean * innov[g : g + 1, :]).astype(jnp.bfloat16)
+        towards = jnp.dot(atm_scaled[slot], there, preferred_element_type=jnp.float32)
+        ocean_out[g : g + 1, :] = jnp.sum(ocean * towards, axis=0, keepdims=True) / (members - 1)
+        towards = jnp.dot(ocean_scaled, back, preferred_element_type=jnp.float32)
+        atm_part = atm[slot].astype(jnp.float32)
+        atm_out[g : g + 1, :] = jnp.sum(atm_part * towards, axis=0, keepdims=True) / (members - 1)
+
+
+def pair_terms(asked, anom, innov, atm, atm_scaled, strips):
+    slots, members, cells = anom.shape
+    whole = lambda i, q: (0, 0, 0)
+    row = pl.BlockSpec((GROUP, cells), lambda i, q: (i, 0))
+    return pl.pallas_call(
+        pair_kernel,
+        grid_spec=pltpu.PrefetchScalarGridSpec(
+            num_scalar_prefetch=1,
+            grid=(slots // GROUP,),
+            in_specs=[
+                pl.BlockSpec((GROUP, members, cells), lambda i, q: (i, 0, 0)),
+                row,
+                pl.BlockSpec(atm.shape, whole),
+                pl.BlockSpec(atm.shape, whole),
+                pl.BlockSpec(strips.shape, whole),
+            ],
+            out_specs=[row, row],
+        ),
+        out_shape=[jax.ShapeDtypeStruct((slots, cells), jnp.float32)] * 2,
+        compiler_params=pltpu.CompilerParams(vmem_limit_bytes=40 * 2**20),
+    )(asked.reshape(-1), anom, innov.astype(jnp.float32), atm, atm_scaled, strips)
 
 
 def local(
@@ -130,26 +179,8 @@
         lax.all_to_all(shipped_innov, "tile", split_axis=0, concat_axis=0, tiled=True),
     )
 
-    def visiting(block_items):
-        anom_rows, innov_rows, asked = block_items
-        tables = jax.vmap(taper_table)(asked[:, 2], asked[:, 3])
-        atm_rows = asked[:, 1]
-        return cross_terms(
-            anom_rows,
-            scaled(anom_rows, innov_rows),
-            atm_anom[atm_rows],
-            atm_scaled[atm_rows],
-            tables,
-        )
-
-    group = math.gcd(slot_total, 64)
-    ocean_terms, atm_terms = lax.map(
-        visiting,
-        (
-            got_anom.reshape(-1, group, members, cell_total),
-            got_innov.reshape(-1, group, cell_total),
-            arrived.reshape(-1, group, 4),
-        ),
+    ocean_terms, atm_terms = pair_terms(
+        arrived, got_anom, got_innov, atm_anom, atm_scaled, taper_strips()
     )
     atm_inc = atm_inc.at[asked_tiles].add(
         atm_terms.reshape(slot_total, cell_total) * slot_live[:, None]

time: 460 us -> 277 us (0.60)
  matrix products: 181 us -> 2.11 us
  Pallas kernels: 0 us -> 19.3 us
  local copies, waits for them, and re-layouts: 49.5 us -> 37.7 us
  waiting for transfers between devices: 153 us -> 142 us
    dot_general x6 -> x0, matrix products: 179 us -> none  [the longest x3 89.5 us: cross_terms(): jnp.einsum('bkj,bij->bki', ocean_weighted, tables, preferred_element_type...]
    pallas_call x0 -> x1, Pallas kernels: none -> 19.3 us  [pair_terms(): pl.pallas_call(pair_kernel, grid_spec=pltpu.PrefetchScalarGridSpec(num_sc...]
    gather x6 -> x0, local copies, waits for them, and re-layouts: 13.7 us -> none  [the longest x3 6.83 us: visiting(): atm_anom[atm_rows]]
    convert_element_type x0 -> x1, other arithmetic: none -> 13.2 us  [taper(): return weight.astype(jnp.bfloat16)]
    dot_general x3 -> x0, other arithmetic: 11.8 us -> none  [cross_terms(): jnp.einsum('bkj,bij->bki', ocean_weighted, tables, preferred_element_type...]
    all_to_all x1, waiting for transfers between devices: 136 us -> 125 us  [local(): lax.all_to_all(shipped, 'tile', split_axis=0, concat_axis=0, tiled=True)]
  transfers between devices with their start and end apart: 6 -> 6, of which waited for: 4 -> 4; matrix products, arithmetic and copies ran while one was open for 8% -> 18% of each run, Pallas kernels for 0% -> 0%
where the time goes in v1:
time: 277 us; the launch traced here: 275 us
  waiting for transfers between devices  142 us (51%)
  starting transfers between devices  52.8 us (19%)
  local copies, waits for them, and re-layouts  37.7 us (14%)
  other arithmetic  20.9 us (8%)
  Pallas kernels  19.3 us (7%)
    all_to_all x1, waiting for transfers between devices, local(): lax.all_to_all(shipped, 'tile', split_axis=0, concat_axis=0, tiled=True)  125 us
    all_to_all x1, starting transfers between devices, local(): lax.all_to_all(ocean_terms.reshape(slot_total, cell_total), 'tile', split...  34.4 us
    scatter x1, local copies, waits for them, and re-layouts, local(): shipped = jnp.zeros((slot_total, members, cell_total), jnp.bfloat16).at[s...  20.5 us
    pallas_call x1, Pallas kernels, pair_terms(): pl.pallas_call(pair_kernel, grid_spec=pltpu.PrefetchScalarGridSpec(num_sc...  19.3 us
    convert_element_type x1, other arithmetic, taper(): return weight.astype(jnp.bfloat16)  13.2 us
    all_to_all x1, waiting for transfers between devices, local(): lax.all_to_all(ocean_terms.reshape(slot_total, cell_total), 'tile', split...  9.89 us
    all_to_all x1, starting transfers between devices, local(): lax.all_to_all(request, 'tile', split_axis=0, concat_axis=0, tiled=True)  7.39 us
    all_to_all x1, starting transfers between devices, local(): lax.all_to_all(shipped, 'tile', split_axis=0, concat_axis=0, tiled=True)  6.18 us
  transfers between devices with their start and end apart: 6, of which 4 were waited for; matrix products, arithmetic and copies ran while one was open for 18% of the time, Pallas kernels for 0%

profile of v1, /device:TPU:0, one launch (start us, length us, event | category | flops | bytes accessed | tf_op | source)
XLA Modules:
  0.0 275.4 jit_solution(651127781538133938)
XLA Ops:
  0.6 0.9 convert_reduce_fusion
  2.2 0.8 pad_add_fusion
  3.1 0.9 scatter_custom_fusion
  4.8 7.4 %all-to-all-start = ((s32[16,12,4]{1,2,0:T(4,128)}), s32[16,12,4]{1,2,0:T(4,128)S(1)}, u32[]{:S(2)}, u32[]{:S(2)}) async-start(s32[16,12,4]{1,2,0:T(4,128)} %copy.32), calls=%async_computation | async-start | bytes 65536 | tf_op jit(solution)/shard_map/all_to_all | solution.py:164
  12.9 2.5 scatter_custom_fusion.2
  16.0 2.8 %all-to-all-done = s32[16,12,4]{1,2,0:T(4,128)S(1)} async-done(((s32[16,12,4]{1,2,0:T(4,128)}), s32[16,12,4]{1,2,0:T(4,128)S(1)}, u32[]{:S(2)}, u32[]{:S(2)}) %all-to-all-start) | async-done | bytes 3104 | tf_op jit(solution)/shard_map/all_to_all | solution.py:164
  18.8 3.5 %all-to-all-start.2 = ((bf16[16,12,256]{2,1,0:T(8,128)(2,1)}), bf16[16,12,256]{2,1,0:T(8,128)(2,1)S(1)}, u32[]{:S(2)}, u32[]{:S(2)}) async-start(bf16[16,12,256]{2,1,0:T(8,128)(2,1)} %all_to_all.29), calls=%async_computation.2 | async-start | bytes 262144 | tf_op jit(solution)/shard_map/all_to_all | solution.py:179
  22.3 4.5 %gather_fusion = bf16[128,80,256]{2,1,0:T(8,128)(2,1)} fusion(bf16[32,80,256]{2,1,0:T(8,128)(2,1)} %param.11, s32[1024]{0:T(1024)S(1)} %pad_clamp_fusion.1), kind=kCustom, calls=%fused_computation | custom fusion | bytes 10486272 | tf_op jit(solution)/shard_map/gather | solution.py:170
  26.8 3.7 %broadcast_in_dim.17 = bf16[192,80,256]{2,1,0:T(8,128)(2,1)} broadcast(bf16[]{:T(256)} %constant.149.clone.1), dimensions={} | broadcast | bytes 7864322 | tf_op jit(solution)/shard_map/broadcast_in_dim | solution.py:168
  30.5 20.5 %scatter_fusion = bf16[192,80,256]{2,1,0:T(8,128)(2,1)} fusion(bf16[192,80,256]{2,1,0:T(8,128)(2,1)} %broadcast_in_dim.17, s32[128]{0:T(128)S(1)} %fusion.70, bf16[128,80,256]{2,1,0:T(8,128)(2,1)} %gather_fusion), kind=kCustom, calls=%fused_computation.4 | custom fusion | bytes 15729152 | tf_op jit(solution)/shard_map/scatter | solution.py:170
  51.0 6.2 %all-to-all-start.1 = ((bf16[192,80,256]{2,1,0:T(8,128)(2,1)}), bf16[192,80,256]{2,1,0:T(8,128)(2,1)}, u32[]{:S(2)}, u32[]{:S(2)}) async-start(bf16[192,80,256]{2,1,0:T(8,128)(2,1)} %scatter_fusion), calls=%async_computation.1 | async-start | bytes 15728640 | tf_op jit(solution)/shard_map/all_to_all | solution.py:178
  57.4 1.1 fusion.13
  58.9 1.1 fusion.11
  60.0 13.2 %fusion.2.strips = bf16[17,512,256]{2,1,0:T(8,128)(2,1)} fusion(s32[256]{0:T(256)S(1)} %and_select_fusion, s32[17,512]{1,0:T(8,128)S(1)} %broadcast_add_fusion, f32[512,256]{1,0:T(8,128)S(1)} %convert_multiply_fusion.4), kind=kLoop, calls=%fused_computation.11 | loop fusion | flops 73531392 | bytes 5016576 | tf_op jit(solution)/shard_map/convert_element_type | solution.py:67
  73.5 125.2 %all-to-all-done.1.anom = bf16[192,80,256]{2,1,0:T(8,128)(2,1)} async-done(((bf16[192,80,256]{2,1,0:T(8,128)(2,1)}), bf16[192,80,256]{2,1,0:T(8,128)(2,1)}, u32[]{:S(2)}, u32[]{:S(2)}) %all-to-all-start.1) | async-done | bytes 7864352 | tf_op jit(solution)/shard_map/all_to_all | solution.py:178
  198.8 2.3 copy-done
  201.0 19.3 %shard_map.122 = (f32[192,256]{1,0:T(8,128)S(1)}, f32[192,256]{1,0:T(8,128)S(1)}) custom-call(s32[768]{0:T(1024)S(1)} %reshape.255.asked, bf16[192,80,256]{2,1,0:T(8,128)(2,1)} %all-to-all-done.1.anom, f32[192,256]{1,0:T(8,128)S(1)} %reshape.258.innov, bf16[32,80,256]{2,1,0:T(8,128)(2,1)S(1)} %copy-done.1, bf16[32,80,256]{2,1,0:T(8,128)(2,1)S(1)} %fusion.10.atm_scaled, ...), custom_call_target="tpu_custom_call" | custom-call | tf_op jit(solution)/shard_map/pallas_call | solution.py:112
  220.3 0.7 all_to_all.31
  221.1 34.4 %all-to-all-start.3 = ((f32[16,12,256]{2,1,0:T(8,128)}), f32[16,12,256]{2,1,0:T(8,128)S(1)}, u32[]{:S(2)}, u32[]{:S(2)}) async-start(f32[16,12,256]{2,1,0:T(8,128)} %all_to_all.31), calls=%async_computation.3 | async-start | bytes 524288 | tf_op jit(solution)/shard_map/all_to_all | solution.py:188
  255.6 9.9 %all-to-all-done.3 = f32[16,12,256]{2,1,0:T(8,128)S(1)} async-done(((f32[16,12,256]{2,1,0:T(8,128)}), f32[16,12,256]{2,1,0:T(8,128)S(1)}, u32[]{:S(2)}, u32[]{:S(2)}) %all-to-all-start.3) | async-done | bytes 196640 | tf_op jit(solution)/shard_map/all_to_all | solution.py:188
  265.5 1.7 scatter_custom_fusion.4
  267.4 1.4 collective-permute-start
  269.0 1.8 scatter_custom_fusion.3
  271.1 3.6 %collective-permute-done.1 = f32[1,512]{1,0:T(1,128)S(1)} collective-permute-done((f32[1,512]{1,0:T(1,128)S(1)}, f32[1,512]{1,0:T(1,128)S(1)}, u32[]{:S(2)}, u32[]{:S(2)}) %collective-permute-start.1) | collective-permute-done | bytes 2080 | tf_op jit(solution)/shard_map/ppermute | solution.py:23
  (59 shorter events, 5.4 us)
Async XLA Ops:
  4.8 14.0 %all-to-all-start = ((s32[16,12,4]{1,2,0:T(4,128)}), s32[16,12,4]{1,2,0:T(4,128)S(1)}, u32[]{:S(2)}, u32[]{:S(2)}) async-start(s32[16,12,4]{1,2,0:T(4,128)} %copy.32), calls=%async_computation | async-start | bytes 65536 | tf_op jit(solution)/shard_map/all_to_all | solution.py:164
  18.8 32.2 %all-to-all-start.2 = ((bf16[16,12,256]{2,1,0:T(8,128)(2,1)}), bf16[16,12,256]{2,1,0:T(8,128)(2,1)S(1)}, u32[]{:S(2)}, u32[]{:S(2)}) async-start(bf16[16,12,256]{2,1,0:T(8,128)(2,1)} %all_to_all.29), calls=%async_computation.2 | async-start | bytes 262144 | tf_op jit(solution)/shard_map/all_to_all | solution.py:179
  51.0 6.2 %copy-start.7 = (bf16[32,256]{1,0:T(8,128)(2,1)S(1)}, bf16[32,256]{1,0:T(8,128)(2,1)}, u32[]{:S(2)}) copy-start(bf16[32,256]{1,0:T(8,128)(2,1)} %param.12) | copy-start | bytes 49156
  51.0 6.2 %copy-start.8 = (bf16[32,256]{1,0:T(8,128)(2,1)S(1)}, bf16[32,256]{1,0:T(8,128)(2,1)}, u32[]{:S(2)}) copy-start(bf16[32,256]{1,0:T(8,128)(2,1)} %param.15) | copy-start | bytes 49156
  51.0 6.4 %copy-start.2 = (bf16[32,80,256]{2,1,0:T(8,128)(2,1)S(1)}, bf16[32,80,256]{2,1,0:T(8,128)(2,1)}, u32[]{:S(2)}) copy-start(bf16[32,80,256]{2,1,0:T(8,128)(2,1)} %param.11) | copy-start | bytes 3932164
  51.0 7.5 %copy-start.3 = (f32[32,256]{1,0:T(8,128)S(1)}, f32[32,256]{1,0:T(8,128)}, u32[]{:S(2)}) copy-start(f32[32,256]{1,0:T(8,128)} %param.13) | copy-start | bytes 98308
  51.0 7.6 %copy-start.1 = (bf16[32,80,256]{2,1,0:T(8,128)(2,1)S(1)}, bf16[32,80,256]{2,1,0:T(8,128)(2,1)}, u32[]{:S(2)}) copy-start(bf16[32,80,256]{2,1,0:T(8,128)(2,1)} %atm.1) | copy-start | bytes 3932164
  51.0 147.8 %all-to-all-start.1 = ((bf16[192,80,256]{2,1,0:T(8,128)(2,1)}), bf16[192,80,256]{2,1,0:T(8,128)(2,1)}, u32[]{:S(2)}, u32[]{:S(2)}) async-start(bf16[192,80,256]{2,1,0:T(8,128)(2,1)} %scatter_fusion), calls=%async_computation.1 | async-start | bytes 15728640 | tf_op jit(solution)/shard_map/all_to_all | solution.py:178
  198.8 2.3 copy-start
  201.0 54.4 %copy-start.4 = (f32[32,256]{1,0:T(8,128)S(1)}, f32[32,256]{1,0:T(8,128)}, u32[]{:S(2)}) copy-start(f32[32,256]{1,0:T(8,128)} %param.16) | copy-start | bytes 98308
  201.0 73.7 %copy-start.5 = (f32[16,512]{1,0:T(8,128)S(1)}, f32[16,512]{1,0:T(8,128)}, u32[]{:S(2)}) copy-start(f32[16,512]{1,0:T(8,128)} %param.17) | copy-start | bytes 98308
  221.1 44.4 %all-to-all-start.3 = ((f32[16,12,256]{2,1,0:T(8,128)}), f32[16,12,256]{2,1,0:T(8,128)S(1)}, u32[]{:S(2)}, u32[]{:S(2)}) async-start(f32[16,12,256]{2,1,0:T(8,128)} %all_to_all.31), calls=%async_computation.3 | async-start | bytes 524288 | tf_op jit(solution)/shard_map/all_to_all | solution.py:188
  267.4 3.6 %collective-permute-start = (f32[1,512]{1,0:T(1,128)S(1)}, f32[1,512]{1,0:T(1,128)S(1)}, u32[]{:S(2)}, u32[]{:S(2)}) collective-permute-start(f32[1,512]{1,0:T(1,128)S(1)} %slice.50), channel_id=1, source_target_pairs={{1,0},{2,1},{3,2},{4,3},{5,4},{6,5},{7,6},{8,7},{9,8},{10,9},{11,1... | collective-permute-start | bytes 6152 | tf_op jit(solution)/shard_map/ppermute | solution.py:24
  269.0 5.7 %collective-permute-start.1 = (f32[1,512]{1,0:T(1,128)S(1)}, f32[1,512]{1,0:T(1,128)S(1)}, u32[]{:S(2)}, u32[]{:S(2)}) collective-permute-start(f32[1,512]{1,0:T(1,128)S(1)} %slice.53), channel_id=1, source_target_pairs={{0,1},{1,2},{2,3},{3,4},{4,5},{5,6},{6,7},{7,8},{8,9},{9,10},{10,1... | collective-permute-start | bytes 6152 | tf_op jit(solution)/shard_map/ppermute | solution.py:23
  270.8 4.6 %copy-start.6 = (f32[32,256]{1,0:T(8,128)}, f32[32,256]{1,0:T(8,128)S(1)}, u32[]{:S(2)}) copy-start(f32[32,256]{1,0:T(8,128)S(1)} %scatter_custom_fusion.3) | copy-start | bytes 98308
